TPU v7x, 256 devices: a whole 4x4x8 slice. The times are simulated.
256 devices in a mesh: seq: 64 (over z, y, core), geo: 4 (over x).
Axes of the slice: x: 4, y: 4, z: 8, core: 2. Of those that a mesh axis runs over, the one named last changes fastest.
Arguments:
- ssm_input: bfloat16 [65536, 768], P(('geo', 'seq')), parts along dimension 0, may hold values from -6 to 6
- gate_input: bfloat16 [65536, 768], P(('geo', 'seq')), parts along dimension 0, may hold values from -6 to 6
- state_proj: bfloat16 [65536, 128], P(('geo', 'seq')), parts along dimension 0, may hold values from -6 to 6
- step_raw: float32 [12, 65536], P(None, ('geo', 'seq')), parts along dimension 1, may hold values from -5 to 5
- decay_log: float32 [12], replicated, may hold values from -20 to 2
- step_bias: float32 [12], replicated, may hold values from -8 to -3
- skip_gain: float32 [12], replicated, may hold values from 0.5 to 1.5
- norm_gain: float32 [768], replicated, may hold values from 0.25 to 1.75
- out_weight: bfloat16 [768, 384], replicated, may hold values from -0.21875 to 0.21875
- block_counts: int32 [256, 64], P('geo'), parts along dimension 0, may hold values from 0 to 2, as said below
- out_cotangent: bfloat16 [65536, 384], P(('geo', 'seq')), parts along dimension 0, may hold values from -6 to 6
Outputs:
- mixed_points: bfloat16 [65536, 384], P(('geo', 'seq')), parts along dimension 0
- grad_input: bfloat16 [65536, 768], P(('geo', 'seq')), parts along dimension 0
- grad_gate: bfloat16 [65536, 768], P(('geo', 'seq')), parts along dimension 0
- grad_proj: bfloat16 [65536, 128], P(('geo', 'seq')), parts along dimension 0
- grad_step: float32 [12, 65536], P(None, ('geo', 'seq')), parts along dimension 1
- grad_weight: float32 [3072, 384], P('geo'), parts along dimension 0
- grad_heads: float32 [12, 12], P('geo'), parts along dimension 0
- grad_norm: float32 [3072], P('geo'), parts along dimension 0
There are 4 independent parts, one for each index of `geo`. A program takes and returns all parts, laid end to end along the dimension named above; an argument that names none is the same for every part. Nothing has to cross between parts.
Inputs may be any that keep to these rules, and one draw needn't show every extreme that they name: block_counts[s, t] is the number of aligned blocks of 128 rows that shard s sends to shard t: symmetric, zero unless s and t differ by at most one, each row sums to 2; entries off the diagonal are at most 1, reached in every draw; shards 0 and 1 exchange exactly 1 block each way.
All inputs are finite; a program needn't handle non-finite values.
Results may differ from a plain program's by a relative error of at most 0.0049.
Values may be sent and summed in bfloat16 or wider, within the bound.
A program may use at most 128 MiB of HBM per device.

v0:
```python
import jax
import jax.numpy as jnp
from jax import lax
from jax.sharding import PartitionSpec as P

BLOCK_ROWS = 128
GROUP = 256


highest = lax.Precision.HIGHEST


def prefix(value, axis, join, neutral, backward):
    count, mine = (lax.axis_size(axis), lax.axis_index(axis))
    pieces = jax.tree.map(lambda part: lax.all_gather(part, axis), value)
    if backward:
        pieces = jax.tree.map(lambda part: part[::-1], pieces)
        mine = count - 1 - mine
    subtotal = jax.tree.map(
        lambda part, zero: jnp.full_like(part, 0) + jnp.asarray(zero, part.dtype), value, neutral
    )

    def lap(position, subtotal):
        longer = join(subtotal, jax.tree.map(lambda part: part[position], pieces))
        return jax.tree.map(lambda new, old: jnp.where(position < mine, new, old), longer, subtotal)

    return lax.fori_loop(0, count - 1, lap, subtotal)


def extended(value, sides, width):
    for axis, dim in sides:
        devices, length = (lax.axis_size(axis), value.shape[dim])
        up = [(i, (i + 1) % devices) for i in range(devices - 1)]
        down = [(j, i) for i, j in up]
        last = lax.slice_in_dim(value, length - width, length, axis=dim)
        initial = lax.slice_in_dim(value, 0, width, axis=dim)
        before = lax.ppermute(last, axis, up)
        after = lax.ppermute(initial, axis, down)
        value = jnp.concatenate([before, value, after], axis=dim)
    return value


def step_decay(step_raw, decay_log, step_bias):
    step_size = jax.nn.softplus(step_raw + step_bias[:, None])
    log_decay = step_size * (-jnp.exp(decay_log))[:, None]
    return (step_size, log_decay)


def gated_norm(y_ssd, gate_f, norm_gain):
    mixed = y_ssd * jax.nn.silu(gate_f)
    inverse_rms = lax.rsqrt(jnp.mean(mixed * mixed, axis=-1, keepdims=True) + 1e-05)
    return mixed * inverse_rms * norm_gain


def ssd_local(ssm_f, proj_f, step_raw, decay_log, step_bias, skip_gain, state_in):
    num_rows, row_width = ssm_f.shape
    head_count = decay_log.shape[0]
    head_dim = row_width // head_count
    state_dim = proj_f.shape[1] // 2
    groups = num_rows // GROUP
    step_size, log_decay = step_decay(step_raw, decay_log, step_bias)
    step_blocks = step_size.reshape(head_count, groups, GROUP)
    cumulative = jnp.cumsum(log_decay.reshape(head_count, groups, GROUP), axis=2)
    x_four = ssm_f.reshape(groups, GROUP, head_count, head_dim)
    b_three = proj_f[:, :state_dim].reshape(groups, GROUP, state_dim)
    c_three = proj_f[:, state_dim:].reshape(groups, GROUP, state_dim)
    positions = jnp.arange(GROUP)
    lower_mask = (positions[:, None] >= positions[None, :])[None, None]
    spread = jnp.where(lower_mask, cumulative[:, :, :, None] - cumulative[:, :, None, :], 0.0)
    weights = jnp.where(lower_mask, jnp.exp(spread), 0.0)
    scores = jnp.einsum("cin,cjn->cij", c_three, b_three, precision=highest)
    mixing = scores[None] * weights * step_blocks[:, :, None, :]
    y_local = jnp.einsum("hcij,cjhp->cihp", mixing, x_four, precision=highest)
    tail_weight = jnp.exp(cumulative[:, :, -1:] - cumulative) * step_blocks
    pieces = jnp.einsum("hcj,cjn,cjhp->chnp", tail_weight, b_three, x_four, precision=highest)
    factor = jnp.exp(cumulative[:, :, -1])
    current = state_in
    entering = [current]
    current = factor[:, 0, None, None] * current + pieces[0]
    y_carry = jnp.einsum("cin,chnp->cihp", c_three, jnp.stack(entering), precision=highest)
    y_carry = y_carry * jnp.exp(cumulative).transpose(1, 2, 0)[..., None]
    y_ssd = (y_local + y_carry).reshape(num_rows, row_width) + ssm_f * jnp.repeat(
        skip_gain, head_dim
    )[None, :]
    return (y_ssd, current)


def chain_combine(earlier, latter):
    return (earlier[0] * latter[0], latter[0][:, None, None] * earlier[1] + latter[1])


def block_order(block_counts, blocks_dev):
    shard_id = lax.axis_index("seq")
    counts_row = lax.dynamic_index_in_dim(block_counts, shard_id, 0, keepdims=False)
    columns = jnp.arange(block_counts.shape[1], dtype=jnp.int32)
    before_count = jnp.sum(jnp.where(columns == shard_id - 1, counts_row, 0))
    after_count = jnp.sum(jnp.where(columns == shard_id + 1, counts_row, 0))
    within = jnp.arange(blocks_dev, dtype=jnp.int32)
    shift = jnp.where(
        within < before_count,
        -before_count,
        jnp.where(within >= blocks_dev - after_count, after_count, 0),
    )
    return blocks_dev // 2 + within + shift


def pick_blocks(padded, block_ids, num_rows):
    return jnp.take(padded, block_ids, axis=0).reshape(num_rows, -1)


def body(
    ssm_input,
    gate_input,
    state_proj,
    step_raw,
    decay_log,
    step_bias,
    skip_gain,
    norm_gain,
    out_weight,
    block_counts,
    out_cotangent,
):
    num_rows, row_width = ssm_input.shape
    head_count = decay_log.shape[0]
    head_dim = row_width // head_count
    state_dim = state_proj.shape[1] // 2
    ssm_f = ssm_input.astype(jnp.float32)
    gate_f = gate_input.astype(jnp.float32)
    proj_f = state_proj.astype(jnp.float32)
    grad_scale = float(num_rows * lax.axis_size("seq")) ** (-0.5)
    zero_state = jnp.zeros((head_count, state_dim, head_dim), jnp.float32)
    y_first, local_state = ssd_local(
        ssm_f, proj_f, step_raw, decay_log, step_bias, skip_gain, zero_state
    )
    _, log_decay = step_decay(step_raw, decay_log, step_bias)
    running = jnp.cumsum(log_decay, axis=1)
    shard_decay = jnp.exp(running[:, -1])
    identity = (jnp.ones_like(shard_decay), jnp.zeros_like(local_state))
    _, state_in = prefix((shard_decay, local_state), "seq", chain_combine, identity, False)
    c_rows = proj_f[:, state_dim:]
    reach = jnp.exp(running).T[:, :, None]
    incoming = jnp.einsum("tn,hnp->thp", c_rows, state_in, precision=highest) * reach
    y_ssd = y_first + incoming.reshape(num_rows, row_width)
    normed_f, norm_pull = jax.vjp(gated_norm, y_ssd, gate_f, norm_gain)
    normed = normed_f.astype(jnp.bfloat16)
    num_blocks = num_rows // BLOCK_ROWS
    half_width = num_blocks // 2
    block_ids = block_order(block_counts, num_blocks)
    contract_cols = (((1,), (1,)), ((), ()))
    contract_rows = (((0,), (0,)), ((), ()))
    out_rows = jnp.dot(normed, out_weight, preferred_element_type=jnp.float32).astype(jnp.bfloat16)
    padded = extended(out_rows.reshape(num_blocks, BLOCK_ROWS, -1), (("seq", 0),), half_width)
    mixed_points = pick_blocks(padded, block_ids, num_rows)
    padded_back = extended(
        out_cotangent.reshape(num_blocks, BLOCK_ROWS, -1), (("seq", 0),), half_width
    )
    returned = pick_blocks(padded_back, block_ids, num_rows)
    g_normed = lax.dot_general(
        returned, out_weight, contract_cols, preferred_element_type=jnp.float32
    )
    weight_term = lax.dot_general(
        normed, returned, contract_rows, preferred_element_type=jnp.float32
    )
    g_yssd, g_gate, g_gain = norm_pull(g_normed)
    g_three = g_yssd.reshape(num_rows, head_count, head_dim) * reach
    back_local = jnp.einsum("tn,thp->hnp", c_rows, g_three, precision=highest)
    _, state_grad = prefix((shard_decay, back_local), "seq", chain_combine, identity, True)

    def local_map(ssm_part, proj_part, step_part, decay_part, bias_part, skip_part):
        return ssd_local(ssm_part, proj_part, step_part, decay_part, bias_part, skip_part, state_in)

    _, ssd_pull = jax.vjp(local_map, ssm_f, proj_f, step_raw, decay_log, step_bias, skip_gain)
    g_ssm, g_proj, g_step, g_decay, g_bias, g_skip = ssd_pull((g_yssd, state_grad))
    head_terms = jnp.stack([g_decay, g_bias, g_skip])
    weight_total, head_total, gain_total = lax.psum((weight_term, head_terms, g_gain), "seq")
    return (
        mixed_points,
        g_ssm.astype(jnp.bfloat16),
        g_gate.astype(jnp.bfloat16),
        g_proj.astype(jnp.bfloat16),
        g_step,
        weight_total * grad_scale,
        head_total * grad_scale,
        gain_total * grad_scale,
    )


def solution(mesh):
    return jax.shard_map(
        body,
        mesh=mesh,
        in_specs=(
            P(("geo", "seq"), None),
            P(("geo", "seq"), None),
            P(("geo", "seq"), None),
            P(None, ("geo", "seq")),
            P(),
            P(),
            P(),
            P(),
            P(),
            P("geo", None),
            P(("geo", "seq"), None),
        ),
        out_specs=(
            P(("geo", "seq"), None),
            P(("geo", "seq"), None),
            P(("geo", "seq"), None),
            P(("geo", "seq"), None),
            P(None, ("geo", "seq")),
            P("geo", None),
            P("geo", None),
            P("geo"),
        ),
        check_vma=False,
    )
```

profile of v0, /device:TPU:1, one launch (start us, length us, event | category | flops | bytes accessed | tf_op | source)
XLA Modules:
  0.0 852.8 jit_solution(9808299870542882503)
XLA Ops:
  13.2 1.3 convolution_add_fusion.1
  14.5 1.6 slice_bitcast_fusion.3
  16.1 4.6 collective-permute-start.2
  20.7 2.5 collective-permute-start.3
  25.8 128.5 %all-reduce.4 = f32[768]{0:T(1024)S(1)} all-reduce(f32[768]{0:T(1024)S(1)} %dynamic-update-slice), channel_id=2, replica_groups=mesh['seq'=64,'geo'=4] {'seq'}, use_global_device_ids=true, to_apply=%add.4 | all-reduce | flops 768 | bytes 6144
  155.9 2.6 fusion.28
  159.6 1.3 fusion.79
  162.2 1.8 compare_and_fusion
  164.7 114.3 %while.28 = (s32[]{:T(128)}, f32[12,64,64]{2,1,0:T(8,128)S(1)}, s32[]{:T(128)}, f32[64,12]{1,0:T(8,128)}, f32[64,12,64,64]{3,2,1,0:T(8,128)}, /*index=5*/s32[]{:T(128)}, s32[]{:T(128)}) while((s32[]{:T(128)}, f32[12,64,64]{2,1,0:T(8,128)S(1)}, s32[]{:T(128)}, f32[64,12]{1,0:T(8,128)}, f32[64,12,64,64]{3,2,1,0:T(8,128)}, ...), condition=%wide.region_5.6_spmd.clone, body=%wide.region_4.5_spmd.clone.sunk | while | flops 196612 | bytes 590073 | solution.py:27
  278.9 1.4 broadcast_multiply_fusion.1
  280.7 1.9 multiply_reduce_fusion.5
  284.4 2.4 collective-permute-start
  286.8 5.9 collective-permute-start.1
  292.7 1.7 pad_maximum_fusion.1
  294.5 2.4 gather_fusion.1
  298.7 1.7 broadcast_select_fusion
  300.4 1.3 multiply_reduce_fusion.2
  301.7 1.5 fusion.88
  303.5 3.1 fusion.33
  309.5 2.3 copy.169
  312.0 1.2 multiply_reduce_fusion.3
  313.3 3.9 fusion.5
  317.2 4.3 fusion.10
  321.5 168.5 %all-reduce.8.cloned.1.call-done = f32[768,384]{1,0:T(8,128)} async-done(((f32[768,384]{1,0:T(8,128)}), f32[768,384]{1,0:T(8,128)}) %all-reduce.8.cloned.1.call-update) | async-done | bytes 1179664 | tf_op jit(solution)/shard_map/psum | solution.py:176
  489.9 2.4 broadcast_multiply_fusion
  492.3 123.4 %all-gather.8.cloned.1.call-done = f32[768,64,64]{2,1,0:T(8,128)} async-done(((f32[12,64,64]{2,1,0:T(8,128)}), f32[768,64,64]{2,1,0:T(8,128)}) %all-gather.8.cloned.1.call-update) | async-done | bytes 12582928 | tf_op jit(solution)/shard_map/all_gather | solution.py:15
  615.7 17.7 %rev.7 = f32[64,12,64,64]{3,2,1,0:T(8,128)} reverse(f32[64,12,64,64]{3,2,1,0:T(8,128)} %bitcast.225), dimensions={0} | reverse | bytes 25165824 | tf_op jit(solution)/shard_map/rev | solution.py:17
  633.4 72.7 %while.29 = (s32[]{:T(128)}, f32[12,64,64]{2,1,0:T(8,128)S(1)}, s32[]{:T(128)}, f32[64,12]{1,0:T(8,128)S(1)}, f32[64,12,64,64]{3,2,1,0:T(8,128)}, /*index=5*/s32[]{:T(128)}, s32[]{:T(128)}) while((s32[]{:T(128)}, f32[12,64,64]{2,1,0:T(8,128)S(1)}, s32[]{:T(128)}, f32[64,12]{1,0:T(8,128)S(1)}, f32[64,12,64,64]{3,2,1,0:T(8,128)}, ...), condition=%wide.region_11.13_spmd.clone, body=%wide.region_10.12_spmd.clone.sunk | while | flops 196612 | bytes 590073 | solution.py:27
  708.2 2.5 reduce-window.26
  711.9 125.7 %all-reduce.5 = (f32[3,12]{1,0:T(4,128)S(1)}, f32[768]{0:T(1024)S(1)}) all-reduce(f32[3,12]{1,0:T(4,128)S(1)} %pad_maximum_fusion.2, f32[768]{0:T(1024)S(1)} %get-tuple-element.287), channel_id=1, replica_groups=mesh['seq'=64,'geo'=4] {'seq'}, use_global_device_ids=true, to_apply=%region_26.28 | all-reduce | flops 804 | bytes 6432 | tf_op jit(solution)/shard_map/psum | solution.py:176
  838.7 2.0 convolution_add_fusion
  841.0 2.1 fusion.93
  (423 shorter events, 209.5 us)
Async XLA Ops:
  7.2 275.4 %copy-start = (bf16[768,384]{1,0:T(8,128)(2,1)S(1)}, bf16[768,384]{1,0:T(8,128)(2,1)}, u32[]{:S(2)}) copy-start(bf16[768,384]{1,0:T(8,128)(2,1)} %param.25) | copy-start | bytes 1769476
  7.2 17.0 %copy-start.32 = (u32[256]{0:T(256)S(1)}, u32[256]{0:T(256)}, u32[]{:S(2)}) copy-start(u32[256]{0:T(256)} %constant.127) | copy-start | bytes 3076
  7.2 147.9 %copy-start.3 = (bf16[256,128]{1,0:T(8,128)(2,1)S(1)}, bf16[256,128]{1,0:T(8,128)(2,1)}, u32[]{:S(2)}) copy-start(bf16[256,128]{1,0:T(8,128)(2,1)} %param.19) | copy-start | bytes 196612
  7.2 157.4 %all-gather.6.cloned.1.call-start = ((), (), s32[]{:S(2)}) async-start(), calls=%async_computation.1 | async-start | bytes 25559040 | tf_op jit(solution)/shard_map/all_gather | solution.py:15
  8.8 149.7 %copy-start.18 = (f32[12,256]{1,0:T(8,128)}, f32[12,256]{1,0:T(8,128)S(1)}, u32[]{:S(2)}) copy-start(f32[12,256]{1,0:T(8,128)S(1)} %get-tuple-element.335) | copy-start | bytes 36868
  10.1 13.1 %copy-start.23 = (f32[12]{0:T(128)}, f32[12]{0:T(128)S(1)}, u32[]{:S(2)}) copy-start(f32[12]{0:T(128)S(1)} %get-tuple-element.292) | copy-start | bytes 148
  11.3 147.2 %copy-start.4 = (bf16[256,768]{0,1:T(8,128)(2,1)}, bf16[256,768]{0,1:T(8,128)(2,1)S(1)}, u32[]{:S(2)}) copy-start(bf16[256,768]{0,1:T(8,128)(2,1)S(1)} %copy.156) | copy-start | bytes 1179652
  13.1 145.4 %copy-start.20 = (f32[12,256]{1,0:T(8,128)}, f32[12,256]{1,0:T(8,128)S(1)}, u32[]{:S(2)}) copy-start(f32[12,256]{1,0:T(8,128)S(1)} %get-tuple-element.326) | copy-start | bytes 36868
  14.4 475.5 %all-reduce.8.cloned.1.call-start = ((), (), s32[]{:S(2)}) async-start(), calls=%async_computation | async-start | bytes 2359296 | tf_op jit(solution)/shard_map/psum | solution.py:176
  16.1 276.6 %collective-permute-start.2 = (bf16[1,128,384]{2,1,0:T(8,128)(2,1)}, bf16[1,128,384]{2,1,0:T(8,128)(2,1)}, u32[]{:S(2)}, u32[]{:S(2)}) collective-permute-start(bf16[1,128,384]{2,1,0:T(8,128)(2,1)} %get-tuple-element.330), channel_id=1, source_target_pairs={{0,4},{4,8},{8,12},{12,16},{16,20},{20,24},{24,28},{28,32},{32,36}... | collective-permute-start | bytes 294920 | tf_op jit(solution)/shard_map/ppermute | solution.py:37
  20.7 272.0 %collective-permute-start.3 = (bf16[1,128,384]{2,1,0:T(8,128)(2,1)}, bf16[1,128,384]{2,1,0:T(8,128)(2,1)}, u32[]{:S(2)}, u32[]{:S(2)}) collective-permute-start(bf16[1,128,384]{2,1,0:T(8,128)(2,1)} %get-tuple-element.331), channel_id=1, source_target_pairs={{4,0},{8,4},{12,8},{16,12},{20,16},{24,20},{28,24},{32,28},{36,32}... | collective-permute-start | bytes 294920 | tf_op jit(solution)/shard_map/ppermute | solution.py:38
  155.1 3.4 copy-start.14
  155.9 2.6 copy-start.11
  155.9 2.9 copy-start.30
  278.9 3.6 copy-start.16
  280.7 16.2 %copy-start.2 = (f32[256,768]{1,0:T(8,128)}, f32[256,768]{1,0:T(8,128)S(1)}, u32[]{:S(2)}) copy-start(f32[256,768]{1,0:T(8,128)S(1)} %copy.163) | copy-start | bytes 2359300
  280.7 12.1 %copy-start.8 = (bf16[256,384]{1,0:T(8,128)(2,1)S(1)}, bf16[256,384]{1,0:T(8,128)(2,1)}, u32[]{:S(2)}) copy-start(bf16[256,384]{1,0:T(8,128)(2,1)} %param.27) | copy-start | bytes 589828
  280.7 18.0 %copy-start.29 = (pred[2]{0:T(512)(128)(4,1)S(1)}, pred[2]{0:T(512)(128)(4,1)}, u32[]{:S(2)}) copy-start(pred[2]{0:T(512)(128)(4,1)} %get-tuple-element.319) | copy-start | bytes 10
  284.4 12.5 %collective-permute-start = (bf16[1,128,384]{2,1,0:T(8,128)(2,1)}, bf16[1,128,384]{2,1,0:T(8,128)(2,1)}, u32[]{:S(2)}, u32[]{:S(2)}) collective-permute-start(bf16[1,128,384]{2,1,0:T(8,128)(2,1)} %get-tuple-element.332), channel_id=1, source_target_pairs={{0,4},{4,8},{8,12},{12,16},{16,20},{20,24},{24,28},{28,32},{32,36}... | collective-permute-start | bytes 294920 | tf_op jit(solution)/shard_map/ppermute | solution.py:37
  286.8 10.0 %collective-permute-start.1 = (bf16[1,128,384]{2,1,0:T(8,128)(2,1)}, bf16[1,128,384]{2,1,0:T(8,128)(2,1)}, u32[]{:S(2)}, u32[]{:S(2)}) collective-permute-start(bf16[1,128,384]{2,1,0:T(8,128)(2,1)} %get-tuple-element.333), channel_id=1, source_target_pairs={{4,0},{8,4},{12,8},{16,12},{20,16},{24,20},{28,24},{32,28},{36,32}... | collective-permute-start | bytes 294920 | tf_op jit(solution)/shard_map/ppermute | solution.py:38
  296.9 6.4 copy-start.26
  303.3 312.5 %all-gather.8.cloned.1.call-start = ((), (), s32[]{:S(2)}) async-start(), calls=%async_computation.2 | async-start | bytes 25559040 | tf_op jit(solution)/shard_map/all_gather | solution.py:15
  306.9 6.3 copy-start.12
  306.9 6.3 copy-start.15
  307.0 6.3 copy-start.19
  307.0 6.3 copy-start.21
  313.3 3.9 copy-start.5
  706.1 4.9 copy-start.28
  706.1 5.7 copy-start.31
  840.7 5.5 copy-start.1
  841.0 4.2 copy-start.10
  843.1 2.1 copy-start.7
  (8 other events, 11.7 us)
Sparse Core Ops, SparseCore 0:
  14.5 126.2 all-gather.5
  303.4 186.4 all-reduce.7
  493.7 122.0 all-gather.7
where the time goes:
time: 861 us; the launch traced here: 853 us
  waiting for transfers between devices  292 us (34%)
  blocking collectives  254 us (30%)
  other arithmetic  168 us (20%)
  local copies, waits for them, and re-layouts  79.8 us (9%)
  matrix products  23.2 us (3%)
  between operations  16.6 us (2%)
  starting transfers between devices  15.6 us (2%)
    psum x1, waiting for transfers between devices, body(): lax.psum((weight_term, head_terms, g_gain), 'seq')  168 us
    select_n x126, other arithmetic, lap(): jnp.where(position < mine, new, old)  140 us
    unnamed x1, blocking collectives  129 us
    psum x1, blocking collectives, body(): lax.psum((weight_term, head_terms, g_gain), 'seq')  126 us
    all_gather x2, waiting for transfers between devices, prefix(): pieces = jax.tree.map(lambda part: lax.all_gather(part, axis), value)  123 us
    mul x126, local copies, waits for them, and re-layouts, chain_combine(): latter[0][:, None, None] * earlier[1] + latter[1]  43.9 us
    rev x2, local copies, waits for them, and re-layouts, prefix(): pieces = jax.tree.map(lambda part: part[::-1], pieces)  17.7 us
  transfers between devices with their start and end apart: 7, of which 2 were waited for; matrix products, arithmetic and copies ran while one was open for 18% of the time, Pallas kernels for 0%

commit v1 on v0

v1 whole, which is shorter than its diff:
```python
import functools

import jax
import jax.numpy as jnp
from jax import lax
from jax.experimental import pallas as pl
from jax.experimental.pallas import tpu as pltpu
from jax.sharding import PartitionSpec as P

ROWS = 256
HEADS = 12
DIN = 768
WIDTH = 384
BLOCK = 128
PLANE = 8
TILES = DIN // 128
f32 = jnp.float32
bf16 = jnp.bfloat16
MESH = pl.DeviceIdType.MESH

FA, FB, FC, BA, BB, BC, RC, RO, W1, W2, W3, W4, W5, W6, HA, HB = range(16)


def mm(a, b):
    return jnp.dot(a, b, preferred_element_type=f32)


def mmt(a, b):
    return lax.dot_general(a, b, (((1,), (1,)), ((), ())), preferred_element_type=f32)


def iota(shape, dim):
    return lax.broadcasted_iota(jnp.int32, shape, dim)


def split2(v):
    hi = v.astype(bf16)
    return hi, (v - hi.astype(f32)).astype(bf16)


def split3(v):
    hi = v.astype(bf16)
    rest = v - hi.astype(f32)
    mid = rest.astype(bf16)
    return hi, mid, (rest - mid.astype(f32)).astype(bf16)


def running(v, ones):
    r = mm(jnp.concatenate(split3(v), axis=0), ones)
    return r[0:16] + r[16:32] + r[32:48]


def softplus(v):
    u = jnp.exp(-jnp.abs(v))
    series = u * (1 - u * (1 / 2 - u * (1 / 3 - u * (1 / 4 - u * (1 / 5 - u * (1 / 6))))))
    return jnp.maximum(v, 0.0) + jnp.where(u < 0.05, series, jnp.log(1 + u))


def kernel(
    nz,
    scale,
    x_ref,
    z_ref,
    bc_ref,
    raw_ref,
    dlog_ref,
    bias_ref,
    skip_ref,
    gain_ref,
    w_ref,
    cnt_ref,
    cot_ref,
    mixed_ref,
    gx_ref,
    gz_ref,
    gp_ref,
    gs_ref,
    gw_ref,
    gh_ref,
    gn_ref,
    pad,
    prow,
    trow,
    colt,
    e768,
    t768,
    txh,
    txl,
    bct,
    swt,
    sc,
    wst,
    mix,
    mixt,
    xm,
    yl,
    sg,
    sgh,
    sgl,
    ret,
    gnorm,
    tmp,
    normed,
    normt,
    gy,
    gb,
    g3h,
    g3l,
    ph,
    plo,
    dsc,
    dsct,
    dxl,
    gpl,
    acc,
    orow,
    wt,
    fa_s,
    fa_r,
    fb_s,
    fb_r,
    fc_s,
    fc_r,
    ba_s,
    ba_r,
    bb_s,
    bb_r,
    bc_s,
    bc_r,
    ent,
    dpre,
    rprev,
    rnext,
    oprev,
    onext,
    w1s,
    w1r,
    w2s,
    w2r,
    w3s,
    w3r,
    w4s,
    w4r,
    w5r,
    w6r,
    ha_s,
    ha_r,
    hb_s,
    hb_r,
    ssem,
    rsem,
):
    shards = PLANE * nz
    nred = w4r.shape[0]
    s = lax.axis_index("seq")
    zi, k = s // PLANE, s % PLANE
    yi, ci = k // 2, k % 2

    barrier = pltpu.get_barrier_semaphore()

    def greet(i):
        pl.semaphore_signal(barrier, inc=1, device_id={"seq": i}, device_id_type=MESH)

    for d in range(1, PLANE):
        greet(zi * PLANE + (k + d) % PLANE)
    for d in range(1, nz):
        greet(((zi + d) % nz) * PLANE + k)
    greet((s + 1) % shards)
    greet((s + shards - 1) % shards)

    def copy(src, dst, phase, d, i):
        return pltpu.make_async_remote_copy(
            src_ref=src,
            dst_ref=dst,
            send_sem=ssem.at[phase, d],
            recv_sem=rsem.at[phase, d],
            device_id={"seq": i},
            device_id_type=MESH,
        )

    def plane_copies(src, dst, phase):
        peers = [(k + d) % PLANE for d in range(1, PLANE)]
        return [
            copy(src(p), dst, phase, d + 1, zi * PLANE + p) for d, p in enumerate(peers)
        ]

    def z_copies(src, dst, phase):
        peers = [(zi + d) % nz for d in range(1, nz)]
        return [copy(src(p), dst, phase, d + 1, p * PLANE + k) for d, p in enumerate(peers)]

    def start(copies):
        for c in copies:
            c.start()

    def wait(copies):
        for c in copies:
            c.wait()

    def state_out(state, send, recv, phase):
        for j in range(PLANE):
            for c in range(TILES):
                send[j, c] = state[8 * j : 8 * j + 8, 128 * c : 128 * c + 128]
        for c in range(TILES):
            prow[c : c + 1, :] = e768[ROWS - 1 : ROWS, 128 * c : 128 * c + 128]
        for j in range(PLANE):
            send[j, TILES] = prow[...]
        recv[k] = send[k]
        copies = plane_copies(lambda p: send.at[p], recv.at[k], phase)
        start(copies)
        return copies

    def scan_plane(recv, send, zrecv, order, phase):
        dp = jnp.ones((8, 128), f32)
        total = [jnp.zeros((8, 128), f32)] * TILES
        for j in order:
            dt = recv[j, TILES]
            dpre[j] = dp
            for c in range(TILES):
                ent[j, c] = total[c]
                total[c] = dt[c : c + 1, :] * total[c] + recv[j, c]
            dp = dp * dt
        for c in range(TILES):
            send[c] = total[c]
        send[TILES] = dp
        zrecv[zi] = send[...]
        copies = z_copies(lambda p: send, zrecv.at[zi], phase)
        start(copies)
        return copies

    def scan_z(zrecv, send, recv, order, takes, phase):
        total = [jnp.zeros((8, 128), f32)] * TILES
        for j in order:
            dt = zrecv[j, TILES]
            use = takes(j)
            for c in range(TILES):
                longer = dt[c : c + 1, :] * total[c] + zrecv[j, c]
                total[c] = jnp.where(use, longer, total[c])
        for j in range(PLANE):
            dp = dpre[j]
            for c in range(TILES):
                send[j, c] = ent[j, c] + dp[c : c + 1, :] * total[c]
        recv[k] = send[k]
        copies = plane_copies(lambda p: send.at[p], recv.at[k], phase)
        start(copies)
        return copies

    def state_in(recv, first):
        for j in range(PLANE):
            for c in range(TILES):
                sg[first + 8 * j : first + 8 * j + 8, 128 * c : 128 * c + 128] = recv[j, c]
        half = pl.ds(first, 64)
        hi, lo = split2(sg[half, :])
        sgh[half, :] = hi
        sgl[half, :] = lo

    head_lane = iota((16, 128), 0) == iota((16, 128), 1)
    prow[...] = jnp.ones((8, 128), f32)
    trow[...] = jnp.zeros((128, ROWS), f32)
    trow[0:1, 0:HEADS] = dlog_ref[...]
    trow[8:9, 0:HEADS] = bias_ref[...]
    trow[16:17, 0:HEADS] = skip_ref[...]
    pad[...] = jnp.zeros((16, ROWS), f32)
    pad[0:HEADS, :] = raw_ref[...]

    def as_column(i):
        return jnp.sum(jnp.where(head_lane, trow[i : i + 1, 0:128], 0.0), axis=1, keepdims=True)

    rate = jnp.exp(as_column(0))
    shifted = pad[...] + as_column(8)
    skip_col = as_column(16)
    owns = iota((16, DIN), 1) // 64 == iota((16, DIN), 0)
    skip_row = jnp.sum(jnp.where(owns, skip_col, 0.0), axis=0, keepdims=True)
    step = softplus(shifted)
    log_decay = -rate * step
    upper = (iota((ROWS, ROWS), 0) <= iota((ROWS, ROWS), 1)).astype(bf16)
    cum = running(log_decay, upper)
    ecum = jnp.exp(cum)
    tail = jnp.exp(cum[:, ROWS - 1 : ROWS] - cum) * step
    pad[...] = step
    trow[0:16, :] = cum
    for first, value in ((16, ecum), (64, tail)):
        for i, part in enumerate(split3(value)):
            trow[first + 16 * i : first + 16 * i + 16, :] = part.astype(f32)
    trow[112:128, :] = jnp.zeros((16, ROWS), f32)
    columns = trow[...].T
    colt[...] = columns
    parts = columns.astype(bf16)
    row_id = iota((128, DIN), 0)
    mine = iota((128, DIN), 1) // 64 == row_id % 16
    e768[...] = mm(parts, (mine & (row_id >= 16) & (row_id < 64)).astype(bf16))
    t768[...] = mm(parts, (mine & (row_id >= 64) & (row_id < 112)).astype(bf16))

    bcf = bc_ref[...].astype(f32)
    bct[...] = bcf.T.astype(bf16)
    lane = iota((ROWS, 128), 1)
    bc_b = jnp.where(lane < 64, bcf, 0.0).astype(bf16)
    bc_c = jnp.where(lane < 64, 0.0, bcf).astype(bf16)

    @pl.loop(0, ROWS // 32)
    def _(i):
        rows = pl.ds(pl.multiple_of(i * 32, 32), 32)
        hi, lo = split2(t768[rows, :] * x_ref[rows, :].astype(f32))
        txh[rows, :] = hi
        txl[rows, :] = lo

    local_state = mm(bct[0:64, :], txh[...]) + mm(bct[0:64, :], txl[...])

    pl.semaphore_wait(barrier, (PLANE - 1) + (nz - 1) + 2)
    fa = state_out(local_state, fa_s, fa_r, FA)
    rc = [
        copy(cot_ref.at[pl.ds(BLOCK, BLOCK), :], rprev, RC, 0, (s + 1) % shards),
        copy(cot_ref.at[pl.ds(0, BLOCK), :], rnext, RC, 1, (s + shards - 1) % shards),
    ]
    start(rc)

    swt[0:64, :] = bct[64:128, :]
    swt[64:128, :] = bct[0:64, :]
    sc[...] = mm(bc_c, swt[...])

    cum_now = trow

    @pl.loop(0, ROWS // 64)
    def _(i):
        first = pl.multiple_of(i * 64, 64)
        rows = pl.ds(first, 64)
        keep = iota((64, ROWS), 0) + first >= iota((64, ROWS), 1)
        score = sc[rows, :]
        col = colt[rows, :]
        for h in range(HEADS):
            spread = col[:, h : h + 1] - cum_now[h : h + 1, :]
            weight = jnp.where(keep, jnp.exp(spread), 0.0) * pad[h : h + 1, :]
            wst[h, rows, :] = weight.astype(bf16)
            mix[h, rows, :] = (weight * score).astype(bf16)

    wait(fa)
    fb = scan_plane(fa_r, fb_s, fb_r, range(PLANE), FB)

    @pl.loop(0, TILES)
    def _(i):
        cols = pl.ds(pl.multiple_of(i * 128, 128), 128)
        both = x_ref[:, cols].astype(f32)
        xm[2 * i] = jnp.where(lane < 64, both, 0.0).astype(bf16)
        xm[2 * i + 1] = jnp.where(lane < 64, 0.0, both).astype(bf16)
        yl[:, cols] = mm(mix[2 * i], xm[2 * i]) + mm(mix[2 * i + 1], xm[2 * i + 1])

    wait(fb)
    fc = scan_z(fb_r, fc_s, fc_r, range(nz), lambda j: j < zi, FC)

    wait(rc)
    count_row = iota(cnt_ref.shape, 0) == s
    count_col = iota(cnt_ref.shape, 1)

    def count(col):
        here = jnp.where(count_row & (count_col == col), cnt_ref[...], 0).astype(f32)
        return jnp.sum(jnp.sum(here, axis=1, keepdims=True), axis=0, keepdims=True)

    from_prev = jnp.broadcast_to(count(s - 1), (BLOCK, WIDTH)) > 0.0
    from_next = jnp.broadcast_to(count(s + 1), (BLOCK, WIDTH)) > 0.0

    def regroup(out, own, prev, following):
        upper_half, lower_half = pl.ds(0, BLOCK), pl.ds(BLOCK, BLOCK)
        out[upper_half, :] = jnp.where(
            from_prev, prev[...].astype(f32), own[upper_half, :].astype(f32)
        ).astype(bf16)
        out[lower_half, :] = jnp.where(
            from_next, following[...].astype(f32), own[lower_half, :].astype(f32)
        ).astype(bf16)

    regroup(ret, cot_ref, rprev, rnext)
    gnorm[...] = mmt(ret[...], w_ref[...])

    @pl.loop(0, HEADS)
    def _(h):
        mixt[h] = mix[h].astype(f32).T.astype(bf16)

    sg[0:64, :] = jnp.zeros((64, DIN), f32)
    sgh[0:64, :] = jnp.zeros((64, DIN), bf16)
    sgl[0:64, :] = jnp.zeros((64, DIN), bf16)
    acc[...] = jnp.zeros(acc.shape, f32)
    gain = gain_ref[...]

    wait(fc)
    state_in(fc_r, 64)
    tmp[...] = mm(bc_c, sgh[...]) + mm(bc_c, sgl[...])

    def by_eight(v):
        return sum(v[8 * i : 8 * i + 8] for i in range(v.shape[0] // 8))

    @pl.loop(0, ROWS // 16)
    def _(i):
        rows = pl.ds(pl.multiple_of(i * 16, 16), 16)
        x = x_ref[rows, :].astype(f32)
        z = z_ref[rows, :].astype(f32)
        local = yl[rows, :]
        reach = e768[rows, :]
        carried = tmp[rows, :]
        y = local + reach * carried + skip_row * x
        sig = 1.0 / (1.0 + jnp.exp(-z))
        silu = z * sig
        u = y * silu
        inv = lax.rsqrt(jnp.mean(u * u, axis=1, keepdims=True) + 1e-5)
        un = u * inv
        normed[rows, :] = (un * gain).astype(bf16)
        g = gnorm[rows, :]
        gg = g * gain
        gu = inv * (gg - un * jnp.mean(gg * un, axis=1, keepdims=True))
        gyv = gu * silu
        gz_ref[rows, :] = (gu * y * (sig * (1.0 + z * (1.0 - sig)))).astype(bf16)
        gyb = gyv.astype(bf16)
        gy[rows, :] = gyv
        gb[rows, :] = gyb
        g3 = gyv * reach
        hi, lo = split2(g3)
        g3h[rows, :] = hi
        g3l[rows, :] = lo
        hi, lo = split2(gyb.astype(f32) * local + g3 * carried)
        ph[rows, :] = hi
        plo[rows, :] = lo
        acc[0:8, :] += by_eight(g * un)
        acc[8:16, :] += by_eight(gyv * x)

    back_local = mm(bct[64:128, :], g3h[...]) + mm(bct[64:128, :], g3l[...])
    ba = state_out(back_local, ba_s, ba_r, BA)

    normt[...] = normed[...].astype(f32).T.astype(bf16)
    twin = zi * PLANE + yi * 2 + (1 - ci)
    theirs = pl.ds(pl.multiple_of((1 - ci) * WIDTH, WIDTH), WIDTH)
    ours = pl.ds(pl.multiple_of(ci * WIDTH, WIDTH), WIDTH)
    w1s[...] = mm(normt[theirs, :], ret[...]).astype(bf16)
    w1 = copy(w1s, w1r, W1, 0, twin)
    w1.start()
    orow[...] = mm(normed[...], w_ref[...]).astype(bf16)
    ro = [
        copy(orow.at[pl.ds(BLOCK, BLOCK), :], oprev, RO, 0, (s + 1) % shards),
        copy(orow.at[pl.ds(0, BLOCK), :], onext, RO, 1, (s + shards - 1) % shards),
    ]
    start(ro)
    wt[...] = mm(normt[ours, :], ret[...])

    wait(ba)
    bb = scan_plane(ba_r, bb_s, bb_r, range(PLANE - 1, -1, -1), BB)

    w1.wait()
    part = WIDTH // 4
    for j in range(4):
        rows = pl.ds(part * j, part)
        w2s[j] = (wt[rows, :] + w1r[rows, :].astype(f32)).astype(bf16)
    w2r[yi] = w2s[yi]
    y_peers = [(yi + d) % 4 for d in range(1, 4)]
    w2 = [
        copy(w2s.at[p], w2r.at[yi], W2, d, zi * PLANE + p * 2 + ci) for d, p in enumerate(y_peers)
    ]
    start(w2)

    @pl.loop(0, ROWS // 64)
    def _(i):
        rows = pl.ds(pl.multiple_of(i * 64, 64), 64)
        total = jnp.zeros((64, ROWS), f32)
        for h in range(HEADS):
            cols = pl.ds(128 * (h // 2), 128)
            total += mmt(gb[rows, cols], xm[h]) * wst[h, rows, :].astype(f32)
        dsc[rows, :] = total

    wait(bb)
    bcx = scan_z(bb_r, bc_s, bc_r, range(nz - 1, -1, -1), lambda j: j > zi, BC)

    @pl.loop(0, TILES)
    def _(i):
        cols = pl.ds(pl.multiple_of(i * 128, 128), 128)
        both = gb[:, cols].astype(f32)
        one = jnp.where(lane < 64, both, 0.0).astype(bf16)
        two = jnp.where(lane < 64, 0.0, both).astype(bf16)
        dxl[:, cols] = mm(mixt[2 * i], one) + mm(mixt[2 * i + 1], two)

    wait(w2)
    rows_z = part // nred
    for j in range(nred):
        rows = pl.ds(rows_z * j, rows_z)
        w3s[j] = sum(w2r[i, rows, :].astype(f32) for i in range(4)).astype(bf16)
    w3 = z_copies(lambda p: w3s.at[p], w3r.at[zi], W3)
    z_peers = [(zi + d) % nz for d in range(1, nz)]
    z_from = [(zi + nz - d) % nz for d in range(1, nz)]
    for c, p in zip(w3, z_peers):

        @pl.when(p < nred)
        def _(c=c):
            c.start()

    swapped = swt[...].astype(f32).T.astype(bf16)
    dsct[...] = dsc[...].T
    dh, dl = split2(dsc[...])
    th, tl = split2(dsct[...])
    gpl[...] = jnp.where(
        lane < 64, mm(th, swapped) + mm(tl, swapped), mm(dh, swapped) + mm(dl, swapped)
    )
    wait(ro)
    regroup(mixed_ref, orow, oprev, onext)

    for c, p in zip(w3, z_peers):

        @pl.when(p < nred)
        def _(c=c):
            c.wait_send()

    w4 = z_copies(lambda p: w4s, w4r.at[zi % nred], W4)

    @pl.when(zi < nred)
    def _():
        for c in w3:
            c.wait_recv()
        w3r[zi] = w3s[zi]
        whole = sum(w3r[i].astype(f32) for i in range(nz)).astype(bf16)
        w4s[...] = whole
        w4r[zi % nred] = whole
        start(w4)

    wait(bcx)
    state_in(bc_r, 0)
    tmp[...] = mm(bc_b, sgh[...]) + mm(bc_b, sgl[...])

    @pl.loop(0, ROWS // 16)
    def _(i):
        rows = pl.ds(pl.multiple_of(i * 16, 16), 16)
        x = x_ref[rows, :].astype(f32)
        far = t768[rows, :] * tmp[rows, :]
        dx = dxl[rows, :] + far
        gx_ref[rows, :] = (dx + skip_row * gy[rows, :]).astype(bf16)
        hi, lo = split2(x * dx)
        txl[rows, :] = hi
        g3l[rows, :] = lo
        acc[16:24, :] += by_eight(x * far)

    select = owns.astype(bf16)
    row_sum = mmt(select, ph[...]) + mmt(select, plo[...])
    col_sum = mmt(select, txl[...]) + mmt(select, g3l[...])

    def per_head(v):
        row = jnp.sum(v, axis=0, keepdims=True)
        return jnp.sum(jnp.where(owns, row, 0.0), axis=1, keepdims=True)

    meet = by_eight(sg[0:64, :] * sg[64:128, :]) * e768[ROWS - 1 : ROWS, :]
    last = per_head(acc[16:24, :] + meet)
    lower = (iota((ROWS, ROWS), 0) >= iota((ROWS, ROWS), 1)).astype(bf16)
    g_log = running(row_sum - col_sum, lower) + last
    g_raw = (col_sum / step - rate * g_log) / (1.0 + jnp.exp(-shifted))
    pad[...] = g_raw
    gs_ref[...] = pad[0:HEADS, :]

    def as_row(col):
        return jnp.sum(jnp.where(head_lane, col, 0.0), axis=0, keepdims=True)

    ha_s[...] = jnp.zeros((16, 128), f32)
    gain_sum = jnp.sum(acc[0:8, :], axis=0, keepdims=True)
    for c in range(TILES):
        ha_s[c : c + 1, :] = gain_sum[:, 128 * c : 128 * c + 128]
    ha_s[8:9, :] = as_row(jnp.sum(g_log * log_decay, axis=1, keepdims=True))
    ha_s[9:10, :] = as_row(jnp.sum(g_raw, axis=1, keepdims=True))
    ha_s[10:11, :] = as_row(per_head(acc[8:16, :]))
    ha_r[k] = ha_s[...]
    ha = plane_copies(lambda p: ha_s, ha_r.at[k], HA)
    start(ha)

    from_t = mmt(txh[...], sgh[...])
    from_g = mmt(g3h[...], sgh[...])
    gp_ref[...] = (gpl[...] + jnp.where(lane < 64, from_t, from_g)).astype(bf16)

    for c, p in zip(w4, z_from):

        @pl.when(p < nred)
        def _(c=c):
            c.wait_recv()

    w5r[yi] = w4r[...]
    w5 = [
        copy(w4r, w5r.at[yi], W5, d, zi * PLANE + p * 2 + ci) for d, p in enumerate(y_peers)
    ]
    start(w5)

    wait(ha)
    hb_s[...] = sum(ha_r[i] for i in range(PLANE))
    hb_r[zi] = hb_s[...]
    hb = z_copies(lambda p: hb_s, hb_r.at[zi], HB)
    start(hb)

    wait(w5)
    w6 = copy(w5r, w6r, W6, 0, twin)
    w6.start()

    def place(first, from_ref):
        for j in range(4):
            for i in range(nred):
                at = pl.multiple_of(first + part * j + rows_z * i, 16)
                gw_ref[pl.ds(at, rows_z), :] = from_ref[j, i].astype(f32) * scale

    place(ci * WIDTH, w5r)
    wait(hb)
    heads = sum(hb_r[i] for i in range(nz)) * scale
    gn_ref[...] = heads[0:TILES, :]
    gh_ref[...] = heads[8:11, 0:HEADS]
    w6.wait()
    place((1 - ci) * WIDTH, w6r)

    @pl.when(zi < nred)
    def _():
        for c in w4:
            c.wait_send()


def body(*args):
    shards = lax.axis_size("seq")
    nz = shards // PLANE
    nred = max(r for r in (1, 2, 3, 6) if r <= nz)
    rows_z = WIDTH // 4 // nred
    ssm, gate, proj, raw, dlog, bias, skip, gain, weight, counts, cot = args
    slots = (PLANE, TILES + 1, 8, 128)
    out = (PLANE, TILES, 8, 128)
    zslots = (nz, TILES + 1, 8, 128)

    def v(shape, dtype):
        return pltpu.VMEM(shape, dtype)

    big, bigh = v((ROWS, DIN), f32), v((ROWS, DIN), bf16)
    square = v((HEADS, ROWS, ROWS), bf16)
    scan = [
        v(slots, f32),
        v(slots, f32),
        v(slots[1:], f32),
        v(zslots, f32),
        v(out, f32),
        v(out, f32),
    ]
    block = v((BLOCK, WIDTH), bf16)
    scratch = [
        v((16, ROWS), f32),
        v((8, 128), f32),
        v((128, ROWS), f32),
        v((ROWS, 128), f32),
        big,
        big,
        bigh,
        bigh,
        v((128, ROWS), bf16),
        v((128, ROWS), bf16),
        v((ROWS, ROWS), f32),
        square,
        square,
        square,
        v((HEADS, ROWS, 128), bf16),
        big,
        v((128, DIN), f32),
        v((128, DIN), bf16),
        v((128, DIN), bf16),
        v((ROWS, WIDTH), bf16),
        big,
        big,
        bigh,
        v((DIN, ROWS), bf16),
        big,
        bigh,
        bigh,
        bigh,
        bigh,
        bigh,
        v((ROWS, ROWS), f32),
        v((ROWS, ROWS), f32),
        big,
        v((ROWS, 128), f32),
        v((24, DIN), f32),
        v((ROWS, WIDTH), bf16),
        v((WIDTH, WIDTH), f32),
        *scan,
        *scan,
        v(out, f32),
        v((PLANE, 8, 128), f32),
        block,
        block,
        block,
        block,
        v((WIDTH, WIDTH), bf16),
        v((WIDTH, WIDTH), bf16),
        v((4, WIDTH // 4, WIDTH), bf16),
        v((4, WIDTH // 4, WIDTH), bf16),
        v((nz, rows_z, WIDTH), bf16),
        v((nz, rows_z, WIDTH), bf16),
        v((rows_z, WIDTH), bf16),
        v((nred, rows_z, WIDTH), bf16),
        v((4, nred, rows_z, WIDTH), bf16),
        v((4, nred, rows_z, WIDTH), bf16),
        v((16, 128), f32),
        v((PLANE, 16, 128), f32),
        v((16, 128), f32),
        v((nz, 16, 128), f32),
        pltpu.SemaphoreType.DMA((16, 8)),
        pltpu.SemaphoreType.DMA((16, 8)),
    ]
    shape = jax.ShapeDtypeStruct
    results = pl.pallas_call(
        functools.partial(kernel, nz, float(ROWS * shards) ** -0.5),
        out_shape=(
            shape((ROWS, WIDTH), bf16),
            shape((ROWS, DIN), bf16),
            shape((ROWS, DIN), bf16),
            shape((ROWS, 128), bf16),
            shape((HEADS, ROWS), f32),
            shape((DIN, WIDTH), f32),
            shape((3, HEADS), f32),
            shape((TILES, 128), f32),
        ),
        in_specs=[pl.BlockSpec(memory_space=pltpu.VMEM)] * 11,
        out_specs=[pl.BlockSpec(memory_space=pltpu.VMEM)] * 8,
        scratch_shapes=scratch,
        compiler_params=pltpu.CompilerParams(
            collective_id=0, has_side_effects=True, vmem_limit_bytes=48 * 2**20
        ),
    )(
        ssm,
        gate,
        proj,
        raw,
        dlog.reshape(1, HEADS),
        bias.reshape(1, HEADS),
        skip.reshape(1, HEADS),
        gain.reshape(1, DIN),
        weight,
        counts,
        cot,
    )
    return (*results[:7], results[7].reshape(DIN))


def solution(mesh):
    rows = P(("geo", "seq"), None)
    cols = P(None, ("geo", "seq"))
    return jax.shard_map(
        body,
        mesh=mesh,
        in_specs=(rows, rows, rows, cols, P(), P(), P(), P(), P(), P("geo", None), rows),
        out_specs=(rows, rows, rows, rows, cols, P("geo", None), P("geo", None), P("geo")),
        check_vma=False,
    )
```

time: 861 us -> 81 us (0.09)
  waiting for transfers between devices: 292 us -> 0 us
  blocking collectives: 254 us -> 0 us
  other arithmetic: 168 us -> 0 us
  Pallas kernels: 0 us -> 65.3 us
  local copies, waits for them, and re-layouts: 79.8 us -> 14.5 us
  matrix products: 23.2 us -> 0 us
  between operations: 16.6 us -> 0.66 us
  starting transfers between devices: 15.6 us -> 0 us
    psum x1 -> x0, waiting for transfers between devices: 168 us -> none  [body(): lax.psum((weight_term, head_terms, g_gain), 'seq')]
    select_n x128 -> x0, other arithmetic: 142 us -> none  [the longest x126 140 us: lap(): jnp.where(position < mine, new, old)]
    unnamed x1 -> x0, blocking collectives: 129 us -> none
    psum x1 -> x0, blocking collectives: 126 us -> none  [body(): lax.psum((weight_term, head_terms, g_gain), 'seq')]
    all_gather x2 -> x0, waiting for transfers between devices: 123 us -> none  [prefix(): pieces = jax.tree.map(lambda part: lax.all_gather(part, axis), value)]
    pallas_call x0 -> x1, Pallas kernels: none -> 65.3 us  [body(): pl.pallas_call(functools.partial(kernel, nz, float(ROWS * shards) ** (-0....]
    mul x131 -> x0, local copies, waits for them, and re-layouts: 48.3 us -> none  [the longest x126 43.9 us: chain_combine(): latter[0][:, None, None] * earlier[1] + latter[1]]
    dot_general x16 -> x0, matrix products: 23.2 us -> none  [the longest x3 10.8 us: ssd_local(): y_local = jnp.einsum('hcij,cjhp->cihp', mixing, x_four, precision=highest)]
  transfers between devices with their start and end apart: 7 -> 0, of which waited for: 2 -> 0; matrix products, arithmetic and copies ran while one was open for 18% -> 0% of each run, Pallas kernels for 0% -> 0%
where the time goes in v1:
time: 81 us; the launch traced here: 80.5 us
  Pallas kernels  65.3 us (81%)
  local copies, waits for them, and re-layouts  14.5 us (18%)
    pallas_call x1, Pallas kernels, body(): pl.pallas_call(functools.partial(kernel, nz, float(ROWS * shards) ** (-0....  65.3 us
    unnamed x28, local copies, waits for them, and re-layouts  13.8 us

profile of v1, /device:TPU:1, one launch (start us, length us, event | category | flops | bytes accessed | tf_op | source)
XLA Modules:
  0.0 80.5 jit_solution(11948705722808393598)
XLA Ops:
  0.6 0.7 reshape.34.gain_ref
  1.3 0.0 copy-start
  1.3 1.1 %copy-done = bf16[768,384]{1,0:T(8,128)(2,1)S(1)} copy-done((bf16[768,384]{1,0:T(8,128)(2,1)S(1)}, bf16[768,384]{1,0:T(8,128)(2,1)}, u32[]{:S(2)}) %copy-start) | copy-done | bytes 589848
  2.4 0.0 copy-start.1
  2.4 1.0 %copy-done.1 = bf16[256,768]{1,0:T(8,128)(2,1)S(1)} copy-done((bf16[256,768]{1,0:T(8,128)(2,1)S(1)}, bf16[256,768]{1,0:T(8,128)(2,1)}, u32[]{:S(2)}) %copy-start.1) | copy-done | bytes 393240
  3.4 0.0 copy-start.2
  3.4 1.0 %copy-done.2 = bf16[256,768]{1,0:T(8,128)(2,1)S(1)} copy-done((bf16[256,768]{1,0:T(8,128)(2,1)S(1)}, bf16[256,768]{1,0:T(8,128)(2,1)}, u32[]{:S(2)}) %copy-start.2) | copy-done | bytes 393240
  4.4 0.0 copy-start.3
  4.4 0.9 %copy-done.3 = bf16[256,384]{1,0:T(8,128)(2,1)S(1)} copy-done((bf16[256,384]{1,0:T(8,128)(2,1)S(1)}, bf16[256,384]{1,0:T(8,128)(2,1)}, u32[]{:S(2)}) %copy-start.3) | copy-done | bytes 196632
  5.3 0.0 copy-start.4
  5.3 0.8 %copy-done.4 = bf16[256,128]{1,0:T(8,128)(2,1)S(1)} copy-done((bf16[256,128]{1,0:T(8,128)(2,1)S(1)}, bf16[256,128]{1,0:T(8,128)(2,1)}, u32[]{:S(2)}) %copy-start.4) | copy-done | bytes 65560
  6.1 0.0 copy-start.5
  6.2 0.8 copy-done.5
  6.9 0.0 copy-start.6
  6.9 0.7 copy-done.6
  7.6 0.0 copy-start.7
  7.6 0.7 copy-done.7
  8.3 0.0 copy-start.8
  8.3 0.7 copy-done.8
  8.9 0.0 copy-start.9
  8.9 0.7 copy-done.9
  9.6 65.3 %shard_map.170 = (bf16[256,384]{1,0:T(8,128)(2,1)S(1)}, bf16[256,768]{1,0:T(8,128)(2,1)S(1)}, bf16[256,768]{1,0:T(8,128)(2,1)S(1)}, bf16[256,128]{1,0:T(8,128)(2...) custom-call(bf16[256,768]{1,0:T(8,128)(2,1)S(1)} %copy-done.1, ...), custom_call_target="tpu_custom_call" | custom-call | tf_op jit(solution)/shard_map/pallas_call | solution.py:697
  74.9 0.7 copy.27
  75.6 0.7 copy.28
  76.4 0.7 copy.29
  77.1 0.6 copy.30
  77.7 0.6 copy.31
  78.4 1.0 %copy.32 = f32[768,384]{1,0:T(8,128)} copy(f32[768,384]{1,0:T(8,128)S(1)} %get-tuple-element.37) | data formatting | bytes 2359296
  79.4 0.6 copy.33
  79.9 0.6 copy.34
Async XLA Ops:
  1.3 1.1 %copy-start = (bf16[768,384]{1,0:T(8,128)(2,1)S(1)}, bf16[768,384]{1,0:T(8,128)(2,1)}, u32[]{:S(2)}) copy-start(bf16[768,384]{1,0:T(8,128)(2,1)} %w_ref.1) | copy-start | bytes 1769476
  2.4 1.0 %copy-start.1 = (bf16[256,768]{1,0:T(8,128)(2,1)S(1)}, bf16[256,768]{1,0:T(8,128)(2,1)}, u32[]{:S(2)}) copy-start(bf16[256,768]{1,0:T(8,128)(2,1)} %x_ref.1) | copy-start | bytes 1179652
  3.4 1.0 %copy-start.2 = (bf16[256,768]{1,0:T(8,128)(2,1)S(1)}, bf16[256,768]{1,0:T(8,128)(2,1)}, u32[]{:S(2)}) copy-start(bf16[256,768]{1,0:T(8,128)(2,1)} %z_ref.1) | copy-start | bytes 1179652
  4.4 0.9 %copy-start.3 = (bf16[256,384]{1,0:T(8,128)(2,1)S(1)}, bf16[256,384]{1,0:T(8,128)(2,1)}, u32[]{:S(2)}) copy-start(bf16[256,384]{1,0:T(8,128)(2,1)} %cot_ref.1) | copy-start | bytes 589828
  5.3 0.8 %copy-start.4 = (bf16[256,128]{1,0:T(8,128)(2,1)S(1)}, bf16[256,128]{1,0:T(8,128)(2,1)}, u32[]{:S(2)}) copy-start(bf16[256,128]{1,0:T(8,128)(2,1)} %bc_ref.1) | copy-start | bytes 196612
  6.1 0.8 copy-start.5
  6.9 0.7 copy-start.6
  7.6 0.7 copy-start.7
  8.3 0.7 copy-start.8
  8.9 0.7 copy-start.9
